TPU v7x, 32 devices: a whole 2x2x4 slice. The times are simulated.
32 devices in a mesh: dp: 4 (over x, core), expert: 4 (over z), head: 2 (over y).
Axes of the slice: x: 2, y: 2, z: 4, core: 2. Of those that a mesh axis runs over, the one named last changes fastest.
Arguments:
- block_input: bfloat16 [16384, 768], P(('dp', 'expert', 'head')), may hold values from -6 to 6
- output_cotangent: bfloat16 [16384, 768], P(('dp', 'expert', 'head')), may hold values from -6 to 6
- token_ids: int32 [16384], P(('dp', 'expert', 'head')), may hold values from 0 to 8007, as said below
- positions: int32 [16384], P(('dp', 'expert', 'head')), may hold values from 0 to 1023, as said below
- hash_table: int32 [8008], replicated, may hold values from 0 to 3, as said below
- first_gain: float32 [768], replicated, may hold values from 0.5 to 1.5
- second_gain: float32 [768], replicated, may hold values from 0.5 to 1.5
- project_weight: bfloat16 [3, 768, 768], P(None, None, 'head'), may hold values from -0.21875 to 0.21875
- output_weight: bfloat16 [768, 768], P('head'), may hold values from -0.875 to 0.875
- expert_inner: bfloat16 [4, 768, 3072], P('expert'), may hold values from -0.21875 to 0.21875
- expert_outer: bfloat16 [4, 3072, 768], P('expert'), may hold values from -0.109375 to 0.109375
Outputs:
- block_output: bfloat16 [16384, 768], P(('dp', 'expert', 'head'))
- input_grad: float32 [16384, 768], P(('dp', 'expert', 'head'))
- first_gain_grad: float32 [768], replicated
- second_gain_grad: float32 [768], replicated
- project_grad: float32 [3, 768, 768], P(None, None, 'head')
- output_weight_grad: float32 [768, 768], P('head')
- expert_inner_grad: float32 [4, 768, 3072], P('expert')
- expert_outer_grad: float32 [4, 3072, 768], P('expert')
Inputs may be any that keep to these rules, and one draw needn't show every extreme that they name: `token_ids`: on every device, exactly 256 of its 512 tokens have ids that hash_table maps to one expert, and at most 256 map to any other expert; within a group of devices along the expert axis this busiest expert is the same for all devices. `hash_table`: every expert is named by 2002 ids. `positions`: documents lie inside sequences of 1024 tokens; the first starts at a sequence's first token; a token's value is its index in the sequence minus that of its document's first token. In every sequence, tokens 1024 // 2 - 1 and 512 share a document. Some sequence is a single document.
All inputs are finite; a program needn't handle non-finite values.
Results may differ from a plain program's by a relative error of at most 0.012.
Values may be sent and summed in bfloat16 or wider, within the bound.
No kernel may reach another device: no remote copies, remote signals or barrier semaphores. Data moves between devices by JAX's collectives and lax.ppermute only.
A program may use at most 256 MiB of HBM per device.

v0:
```python
import jax
import jax.numpy as jnp
from jax import lax
from jax.sharding import PartitionSpec as P

HEAD_DIM = 64


def layer_norm(values, gain):
    center = values - jnp.mean(values, axis=-1, keepdims=True)
    spread = jnp.mean(center * center, axis=-1, keepdims=True)
    return center * lax.rsqrt(spread + 1e-05) * gain


def sum_experts(inner_part, outer_part):
    return lax.psum((inner_part, outer_part), ("dp", "head"))


def on_device(
    block_input,
    output_cotangent,
    token_ids,
    positions,
    hash_table,
    first_gain,
    second_gain,
    project_weight,
    output_weight,
    expert_inner,
    expert_outer,
):
    tok_rows = block_input.shape[0]
    model_width = block_input.shape[1]
    local_cols = output_weight.shape[0]
    head_count = local_cols // HEAD_DIM
    expert_count = lax.axis_size("expert")
    capacity = tok_rows // 2
    inner_weight = expert_inner[0]
    outer_weight = expert_outer[0]
    residual = block_input.astype(jnp.float32)
    first_low = layer_norm(residual, first_gain).astype(jnp.bfloat16)
    gathered, seq_pos = (
        lax.all_gather(first_low, "head", axis=0, tiled=True),
        lax.all_gather(positions, "head", axis=0, tiled=True),
    )
    seq_len = gathered.shape[0]
    projected = jnp.einsum(
        "td,cde->cte", gathered, project_weight, preferred_element_type=jnp.float32
    ).astype(jnp.bfloat16)
    head_values = projected.reshape(3, seq_len, head_count, HEAD_DIM)
    ordering = jnp.arange(seq_len, dtype=jnp.int32)
    visible = (ordering[None, :] <= ordering[:, None]) & (
        ordering[None, :] >= (ordering - seq_pos)[:, None]
    )
    scores = (
        jnp.einsum(
            "qhd,khd->hqk", head_values[0], head_values[1], preferred_element_type=jnp.float32
        )
        * 0.125
    )
    scores = jnp.where(visible[None], scores, -1000000000.0)
    row_max = jnp.max(scores, axis=-1, keepdims=True)
    exponent = jnp.exp(scores - row_max)
    row_total = jnp.sum(exponent, axis=-1, keepdims=True)
    log_total = row_max + jnp.log(row_total)
    probabilities = (exponent / row_total).astype(jnp.bfloat16)
    context = jnp.einsum(
        "hqk,khd->qhd", probabilities, head_values[2], preferred_element_type=jnp.float32
    )
    context = context.astype(jnp.bfloat16).reshape(seq_len, local_cols)
    row_block = context
    attended = lax.psum_scatter(
        jnp.dot(row_block, output_weight, preferred_element_type=jnp.float32),
        "head",
        scatter_dimension=0,
        tiled=True,
    )
    hidden = residual + attended
    second_low = layer_norm(hidden, second_gain).astype(jnp.bfloat16)
    chosen = jnp.take(hash_table, token_ids)
    one_hot = chosen[:, None] == jnp.arange(expert_count, dtype=jnp.int32)[None, :]
    rank_table = jnp.cumsum(one_hot.astype(jnp.int32), axis=0) - 1
    slot_index = chosen * capacity + jnp.sum(jnp.where(one_hot, rank_table, 0), axis=1)
    outgoing = (
        jnp.zeros((expert_count * capacity, model_width), jnp.bfloat16)
        .at[slot_index]
        .set(second_low)
    )
    outgoing = outgoing.reshape(expert_count, capacity, model_width)
    arrived = lax.all_to_all(outgoing, "expert", split_axis=0, concat_axis=0, tiled=True)
    pre_act = jnp.einsum("scd,df->scf", arrived, inner_weight, preferred_element_type=jnp.float32)
    activated = jax.nn.gelu(pre_act).astype(jnp.bfloat16)
    produced = jnp.einsum(
        "scf,fd->scd", activated, outer_weight, preferred_element_type=jnp.float32
    )
    produced, arrived_rows = (produced.astype(jnp.bfloat16), arrived)
    combined = lax.all_to_all(produced, "expert", split_axis=0, concat_axis=0, tiled=True).reshape(
        expert_count * capacity, model_width
    )
    block_output = (hidden + combined[slot_index].astype(jnp.float32)).astype(jnp.bfloat16)
    cotangent = output_cotangent.astype(jnp.float32)
    grad_out = (
        jnp.zeros((expert_count * capacity, model_width), jnp.bfloat16)
        .at[slot_index]
        .set(output_cotangent)
    )
    grad_out = grad_out.reshape(expert_count, capacity, model_width)
    grad_arrived = lax.all_to_all(grad_out, "expert", split_axis=0, concat_axis=0, tiled=True)
    pre_act = jnp.einsum(
        "scd,df->scf", arrived_rows, inner_weight, preferred_element_type=jnp.float32
    )
    activated = jax.nn.gelu(pre_act).astype(jnp.bfloat16)
    outer_grad = jnp.einsum(
        "scf,scd->fd", activated, grad_arrived, preferred_element_type=jnp.float32
    )
    act_grad = jnp.einsum(
        "scd,fd->scf", grad_arrived, outer_weight, preferred_element_type=jnp.float32
    )
    pre_grad = jax.vjp(jax.nn.gelu, pre_act)[1](act_grad)[0].astype(jnp.bfloat16)
    inner_grad = jnp.einsum(
        "scd,scf->df", arrived_rows, pre_grad, preferred_element_type=jnp.float32
    )
    rows_grad = jnp.einsum(
        "scf,df->scd", pre_grad, inner_weight, preferred_element_type=jnp.float32
    ).astype(jnp.bfloat16)
    returned_grad = lax.all_to_all(
        rows_grad, "expert", split_axis=0, concat_axis=0, tiled=True
    ).reshape(expert_count * capacity, model_width)
    second_grad = returned_grad[slot_index].astype(jnp.float32)
    second_back = jax.vjp(layer_norm, hidden, second_gain)[1]
    hidden_part, second_gain_part = second_back(second_grad)
    hidden_grad = cotangent + hidden_part
    shard_rows = lax.all_gather(hidden_grad.astype(jnp.bfloat16), "head", axis=0, tiled=True)
    grad_piece = jnp.einsum(
        "td,cd->tc", shard_rows, output_weight, preferred_element_type=jnp.float32
    )
    row_block = context
    weight_run = jnp.einsum("tc,td->cd", row_block, shard_rows, preferred_element_type=jnp.float32)
    context_grad = grad_piece
    context_grad = context_grad.astype(jnp.bfloat16).reshape(seq_len, head_count, HEAD_DIM)
    scores = (
        jnp.einsum(
            "qhd,khd->hqk", head_values[0], head_values[1], preferred_element_type=jnp.float32
        )
        * 0.125
    )
    scores = jnp.where(visible[None], scores, -1000000000.0)
    soft = jnp.exp(scores - log_total)
    value_grad = jnp.einsum(
        "hqk,qhd->khd", soft.astype(jnp.bfloat16), context_grad, preferred_element_type=jnp.float32
    ).astype(jnp.bfloat16)
    prob_grad = jnp.einsum(
        "qhd,khd->hqk", context_grad, head_values[2], preferred_element_type=jnp.float32
    )
    inner_sum = jnp.sum(soft * prob_grad, axis=-1, keepdims=True)
    score_grad = (soft * (prob_grad - inner_sum)).astype(jnp.bfloat16)
    query_grad = (
        jnp.einsum("hqk,khd->qhd", score_grad, head_values[1], preferred_element_type=jnp.float32)
        * 0.125
    ).astype(jnp.bfloat16)
    key_grad = (
        jnp.einsum("hqk,qhd->khd", score_grad, head_values[0], preferred_element_type=jnp.float32)
        * 0.125
    ).astype(jnp.bfloat16)
    mixed_grad = jnp.stack([query_grad, key_grad, value_grad]).reshape(3, seq_len, local_cols)
    project_part = jnp.einsum(
        "td,cte->cde", gathered, mixed_grad, preferred_element_type=jnp.float32
    )
    first_grad = lax.psum_scatter(
        jnp.einsum("cte,cde->td", mixed_grad, project_weight, preferred_element_type=jnp.float32),
        "head",
        scatter_dimension=0,
        tiled=True,
    )
    first_back = jax.vjp(layer_norm, residual, first_gain)[1]
    input_part, first_gain_part = first_back(first_grad)
    input_grad = hidden_grad + input_part
    first_gain_grad, second_gain_grad = lax.psum(
        (first_gain_part, second_gain_part), ("dp", "expert", "head")
    )
    project_grad, output_weight_grad = lax.psum((project_part, weight_run), ("dp", "expert"))
    inner_total, outer_total = sum_experts(inner_grad, outer_grad)
    return (
        block_output,
        input_grad,
        first_gain_grad,
        second_gain_grad,
        project_grad,
        output_weight_grad,
        inner_total[None],
        outer_total[None],
    )


def solution(mesh):
    in_specs = (
        P(("dp", "expert", "head"), None),
        P(("dp", "expert", "head"), None),
        P(("dp", "expert", "head")),
        P(("dp", "expert", "head")),
        P(),
        P(),
        P(),
        P(None, None, "head"),
        P("head", None),
        P("expert", None, None),
        P("expert", None, None),
    )
    out_specs = (
        P(("dp", "expert", "head"), None),
        P(("dp", "expert", "head"), None),
        P(),
        P(),
        P(None, None, "head"),
        P("head", None),
        P("expert", None, None),
        P("expert", None, None),
    )
    return jax.shard_map(
        on_device, mesh=mesh, in_specs=in_specs, out_specs=out_specs, check_vma=False
    )
```

profile of v0, /device:TPU:0, one launch (start us, length us, event | category | flops | bytes accessed | tf_op | source)
XLA Modules:
  0.0 832.1 jit_solution(18277433671254045007)
XLA Ops:
  13.8 5.3 all-gather
  19.6 24.2 %all-gather.4.cloned.1.call-done = bf16[1024,768]{1,0:T(8,128)(2,1)} async-done(((bf16[512,768]{1,0:T(8,128)(2,1)}), bf16[1024,768]{1,0:T(8,128)(2,1)}) %all-gather.4.cloned.1.call-update) | async-done | bytes 1572880 | tf_op jit(solution)/shard_map/all_gather | solution.py:43
  47.5 10.7 %fusion.69 = (f32[6,1024]{1,0:T(8,128)S(1)}, f32[6,1024,1024]{1,2,0:T(8,128)}) fusion(bf16[1024,6,64]{0,2,1:T(8,128)(2,1)S(1)} %bitcast.101, bf16[1024,6,64]{0,2,1:T(8,128)(2,1)S(1)} %bitcast.99, pred[1024,1024]{0,1:T(8,128)(4,1)S(1)} %fusion.21), kind=kOutput, calls=%fused_computation.117 | convolution fusion | flops 824174592 | bytes 27811840 | tf_op jit(solution)/shard_map/qhd,khd->hqk/dot_general | solution.py:56
  58.2 10.2 %fusion = f32[6,1024]{1,0:T(8,128)S(1)} fusion(f32[6,1024,1024]{1,2,0:T(8,128)} %get-tuple-element.51, f32[6,1024]{1,0:T(8,128)S(1)} %get-tuple-element.50), kind=kLoop, calls=%fused_computation.11 | loop fusion | flops 12576768 | bytes 25214976 | tf_op jit(solution)/shard_map/reduce_sum | solution.py:64
  68.4 10.5 %fusion.49 = bf16[6,64,1024]{2,1,0:T(8,128)(2,1)S(1)} fusion(bf16[1024,6,64]{0,2,1:T(8,128)(2,1)S(1)} %bitcast.112, f32[6,1024,1024]{1,2,0:T(8,128)} %get-tuple-element.51, f32[6,1024]{1,0:T(8,128)S(1)} %fusion, f32[6,1024]{1,0:T(8,128)S(1)} %get-tuple-element.50), kind=kOutput, calls=%fused_computation.77 | convolution fusion | flops 824573952 | bytes 26787840 | tf_op jit(solution)/shard_map/hqk,khd->qhd/dot_general | solution.py:67
  88.3 37.8 %reduce-scatter.3.cloned.1.call-done = f32[512,768]{1,0:T(8,128)} async-done(((f32[1024,768]{1,0:T(8,128)}), f32[512,768]{1,0:T(8,128)}) %reduce-scatter.3.cloned.1.call-update) | async-done | bytes 1572880 | tf_op jit(solution)/shard_map/reduce_scatter | solution.py:72
  132.2 4.8 all-to-all-start
  141.4 32.7 %all-to-all-done = bf16[4,256,768]{2,1,0:T(8,128)(2,1)} async-done(((bf16[4,256,768]{2,1,0:T(8,128)(2,1)}), bf16[4,256,768]{2,1,0:T(8,128)(2,1)}, u32[]{:S(2)}, u32[]{:S(2)}) %all-to-all-start) | async-done | bytes 1572896 | tf_op jit(solution)/shard_map/all_to_all | solution.py:90
  178.5 7.4 fusion.19
  190.3 10.8 %fusion.35 = bf16[4,256,768]{2,1,0:T(8,128)(2,1)} fusion(bf16[1,3072,768]{2,1,0:T(8,128)(2,1)} %param.21, f32[4,256,3072]{2,1,0:T(8,128)S(1)} %fusion.19), kind=kOutput, calls=%fused_computation.59 | convolution fusion | flops 4860936192 | bytes 18874368 | tf_op jit(solution)/shard_map/scf,fd->scd/dot_general | solution.py:93
  201.1 13.9 %all-to-all-done.2 = bf16[4,256,768]{2,1,0:T(8,128)(2,1)} async-done(((bf16[4,256,768]{2,1,0:T(8,128)(2,1)}), bf16[4,256,768]{2,1,0:T(8,128)(2,1)}, u32[]{:S(2)}, u32[]{:S(2)}) %all-to-all-start.2) | async-done | bytes 1572896 | tf_op jit(solution)/shard_map/all_to_all | solution.py:108
  215.0 4.8 all-to-all-start.1
  219.8 15.3 %fusion.8 = bf16[4,256,3072]{2,1,0:T(8,128)(2,1)S(1)} fusion(f32[4,256,3072]{2,1,0:T(8,128)} %copy-done.31, bf16[4,256,768]{2,1,0:T(8,128)(2,1)} %all-to-all-done.2, bf16[1,3072,768]{2,1,0:T(8,128)(2,1)} %param.21), kind=kOutput, calls=%fused_computation.21 | convolution fusion | flops 4894752768 | bytes 25165824 | tf_op jit(solution)/shard_map/scd,fd->scf/dot_general | solution.py:116
  237.9 8.5 %fusion.32 = bf16[4,256,768]{2,1,0:T(8,128)(2,1)} fusion(bf16[4,256,3072]{2,1,0:T(8,128)(2,1)S(1)} %fusion.8, bf16[1,768,3072]{2,1,0:T(8,128)(2,1)} %param.20), kind=kOutput, calls=%fused_computation.58 | convolution fusion | flops 4832624640 | bytes 12582912 | tf_op jit(solution)/shard_map/scf,df->scd/dot_general | solution.py:123
  246.4 9.9 %all-to-all-done.1 = bf16[4,256,768]{2,1,0:T(8,128)(2,1)} async-done(((bf16[4,256,768]{2,1,0:T(8,128)(2,1)}), bf16[4,256,768]{2,1,0:T(8,128)(2,1)}, u32[]{:S(2)}, u32[]{:S(2)}) %all-to-all-start.1) | async-done | bytes 1572896 | tf_op jit(solution)/shard_map/all_to_all | solution.py:97
  260.7 4.7 gather_fusion.1
  265.4 31.8 %all-to-all-done.3 = bf16[4,256,768]{2,1,0:T(8,128)(2,1)} async-done(((bf16[4,256,768]{2,1,0:T(8,128)(2,1)}), bf16[4,256,768]{2,1,0:T(8,128)(2,1)}, u32[]{:S(2)}, u32[]{:S(2)}) %all-to-all-start.3) | async-done | bytes 1572896 | tf_op jit(solution)/shard_map/all_to_all | solution.py:126
  297.2 4.7 gather_fusion.2
  308.1 25.3 %all-gather.6.cloned.1.call-done = bf16[1024,768]{1,0:T(8,128)(2,1)} async-done(((bf16[512,768]{1,0:T(8,128)(2,1)}), bf16[1024,768]{1,0:T(8,128)(2,1)}) %all-gather.6.cloned.1.call-update) | async-done | bytes 1572880 | tf_op jit(solution)/shard_map/all_gather | solution.py:133
  335.6 11.2 %fusion.46 = bf16[6,64,1024]{2,1,0:T(8,128)(2,1)} fusion(bf16[1024,6,64]{0,2,1:T(8,128)(2,1)S(1)} %bitcast.108, f32[6,1024,1024]{1,2,0:T(8,128)} %get-tuple-element.51, f32[6,1024]{1,0:T(8,128)S(1)} %log_add_fusion), kind=kOutput, calls=%fused_computation.76 | convolution fusion | flops 818282496 | bytes 26763264 | tf_op jit(solution)/shard_map/hqk,qhd->khd/dot_general | solution.py:149
  346.8 15.5 %multiply_reduce_fusion = (f32[6,1024]{1,0:T(8,128)S(1)}, f32[6,1024,1024]{1,2,0:T(8,128)}) fusion(f32[6,1024,1024]{1,2,0:T(8,128)} %get-tuple-element.51, f32[6,1024]{1,0:T(8,128)S(1)} %log_add_fusion, bf16[1024,6,64]{0,2,1:T(8,128)(2,1)S(1)} %bitcast.109, bf16[1024,6,64]{0,2,1:T(8,128)(2,1)S(1)} %bitcast.113), kind=kOutput, calls=%fused_computation.6 | convolution fusion | flops 824174592 | bytes 51953664 | tf_op jit(solution)/shard_map/qhd,khd->hqk/dot_general | solution.py:152
  362.4 16.8 %multiply_convert_fusion = bf16[6,1024,1024]{1,2,0:T(8,128)(2,1)S(1)} fusion(f32[6,1024,1024]{1,2,0:T(8,128)} %get-tuple-element.53, f32[6,1024,1024]{1,2,0:T(8,128)} %get-tuple-element.51, f32[6,1024]{1,0:T(8,128)S(1)} %get-tuple-element.52, f32[6,1024]{1,0:T(8,128)S(1)} %log_add_fusion), kind=kLoop, calls=%fused_computation.5 | loop fusion | flops 25165824 | bytes 62963712 | tf_op jit(solution)/shard_map/convert_element_type | solution.py:156
  379.2 5.9 multiply_convert_fusion.2
  402.1 5.1 convolution_bitcast_fusion.3
  407.2 10.2 %convolution_bitcast_fusion.1 = f32[1,768,3072]{2,1,0:T(8,128)} fusion(bf16[4,256,768]{2,1,0:T(8,128)(2,1)} %all-to-all-done, bf16[4,256,3072]{2,1,0:T(8,128)(2,1)} %copy-done.30), kind=kOutput, calls=%fused_computation.27 | convolution fusion | flops 4831838208 | bytes 17301504 | tf_op jit(solution)/shard_map/scd,scf->df/dot_general | solution.py:120
  417.4 12.9 %convolution_bitcast_fusion = f32[1,3072,768]{2,1,0:T(8,128)} fusion(bf16[4,256,768]{2,1,0:T(8,128)(2,1)} %all-to-all-done.2, f32[4,256,3072]{2,1,0:T(8,128)} %copy-done.31), kind=kOutput, calls=%fused_computation.26 | convolution fusion | flops 4860149760 | bytes 23592960 | tf_op jit(solution)/shard_map/scf,scd->fd/dot_general | solution.py:113
  430.3 89.0 %all-reduce.6.cloned.1.call-done = (f32[3,768,384]{1,2,0:T(8,128)}, f32[384,768]{1,0:T(8,128)}) async-done(((f32[3,768,384]{1,2,0:T(8,128)}, f32[384,768]{1,0:T(8,128)}), (f32[3,768,384]{1,2,0:T(8,128)}, f32[384,768]{1,0:T(8,128)})) %all-reduce.6.cloned.1.call-update) | async-done | bytes 4718608 | tf_op jit(solution)/shard_map/psum | solution.py:181
  519.4 5.2 copy.54
  524.6 40.2 %reduce-scatter.5.cloned.1.call-done = f32[512,768]{1,0:T(8,128)} async-done(((f32[1024,768]{1,0:T(8,128)}), f32[512,768]{1,0:T(8,128)}) %reduce-scatter.5.cloned.1.call-update) | async-done | bytes 1572880 | tf_op jit(solution)/shard_map/reduce_scatter | solution.py:169
  567.6 40.1 %all-reduce = (f32[768]{0:T(1024)}, f32[768]{0:T(1024)}) all-reduce(f32[768]{0:T(1024)S(1)} %get-tuple-element.32, f32[768]{0:T(1024)S(1)} %get-tuple-element.34), channel_id=1, replica_groups=mesh['dp'=4,'expert'=4,'head'=2] {'dp','expert','head'}, use_global_device_ids=true, to_apply=%region_19.20 | all-reduce | flops 1536 | bytes 12288 | tf_op jit(solution)/shard_map/psum | solution.py:178
  611.5 198.5 %all-reduce.8.cloned.1.call-done = (f32[1,768,3072]{2,1,0:T(8,128)}, f32[1,3072,768]{2,1,0:T(8,128)}) async-done(((f32[1,768,3072]{2,1,0:T(8,128)}, f32[1,3072,768]{2,1,0:T(8,128)}), (f32[1,768,3072]{2,1,0:T(8,128)}, f32[1,3072,768]{2,1,0:T(8,128)})) %all-reduce.8.cloned.1.call-update) | async-done | bytes 18874384 | tf_op jit(solution)/shard_map/psum | solution.py:16
  812.5 8.8 %copy.70 = f32[1,768,3072]{2,1,0:T(8,128)} copy(f32[1,768,3072]{2,1,0:T(8,128)} %get-tuple-element.60) | data formatting | bytes 18874368
  (133 shorter events, 84.6 us)
Async XLA Ops:
  7.2 36.6 %copy-start = (bf16[3,768,384]{2,1,0:T(8,128)(2,1)S(1)}, bf16[3,768,384]{2,1,0:T(8,128)(2,1)}, u32[]{:S(2)}) copy-start(bf16[3,768,384]{2,1,0:T(8,128)(2,1)} %param.18) | copy-start | bytes 5308420
  7.2 6.6 copy-start.28
  7.2 36.6 %all-gather.4.cloned.1.call-start = ((), (), s32[]{:S(2)}) async-start(), calls=%async_computation.6 | async-start | bytes 2359296 | tf_op jit(solution)/shard_map/all_gather | solution.py:43
  13.7 112.4 %reduce-scatter.3.cloned.1.call-start = ((), (), s32[]{:S(2)}) async-start(), calls=%async_computation.7 | async-start | bytes 4718592 | tf_op jit(solution)/shard_map/reduce_scatter | solution.py:72
  47.4 10.8 %copy-start.5 = (bf16[1,1024,384]{1,2,0:T(8,128)(2,1)}, bf16[1,1024,384]{1,2,0:T(8,128)(2,1)S(1)}, u32[]{:S(2)}) copy-start(bf16[1,1024,384]{1,2,0:T(8,128)(2,1)S(1)} %get-tuple-element.46) | copy-start | bytes 2359300
  47.5 10.7 %copy-start.6 = (bf16[1,1024,384]{1,2,0:T(8,128)(2,1)}, bf16[1,1024,384]{1,2,0:T(8,128)(2,1)S(1)}, u32[]{:S(2)}) copy-start(bf16[1,1024,384]{1,2,0:T(8,128)(2,1)S(1)} %get-tuple-element.47) | copy-start | bytes 2359300
  47.5 20.9 %copy-start.12 = (bf16[1,1024,384]{1,2,0:T(8,128)(2,1)}, bf16[1,1024,384]{1,2,0:T(8,128)(2,1)S(1)}, u32[]{:S(2)}) copy-start(bf16[1,1024,384]{1,2,0:T(8,128)(2,1)S(1)} %get-tuple-element.48) | copy-start | bytes 2359300
  68.4 11.5 %copy-start.17 = (bf16[384,768]{1,0:T(8,128)(2,1)S(1)}, bf16[384,768]{1,0:T(8,128)(2,1)}, u32[]{:S(2)}) copy-start(bf16[384,768]{1,0:T(8,128)(2,1)} %param.19) | copy-start | bytes 1769476
  88.3 40.0 %copy-start.22 = (f32[768]{0:T(1024)S(1)}, f32[768]{0:T(1024)}, u32[]{:S(2)}) copy-start(f32[768]{0:T(1024)} %param.17) | copy-start | bytes 9220
  132.2 41.9 %all-to-all-start = ((bf16[4,256,768]{2,1,0:T(8,128)(2,1)}), bf16[4,256,768]{2,1,0:T(8,128)(2,1)}, u32[]{:S(2)}, u32[]{:S(2)}) async-start(bf16[4,256,768]{2,1,0:T(8,128)(2,1)} %bitcast.106), calls=%async_computation.1 | async-start | bytes 3145728 | tf_op jit(solution)/shard_map/all_to_all | solution.py:90
  174.1 40.9 %all-to-all-start.2 = ((bf16[4,256,768]{2,1,0:T(8,128)(2,1)}), bf16[4,256,768]{2,1,0:T(8,128)(2,1)}, u32[]{:S(2)}, u32[]{:S(2)}) async-start(bf16[4,256,768]{2,1,0:T(8,128)(2,1)} %bitcast.105), calls=%async_computation.3 | async-start | bytes 3145728 | tf_op jit(solution)/shard_map/all_to_all | solution.py:108
  185.8 4.5 copy-start.31
  215.0 41.3 %all-to-all-start.1 = ((bf16[4,256,768]{2,1,0:T(8,128)(2,1)}), bf16[4,256,768]{2,1,0:T(8,128)(2,1)}, u32[]{:S(2)}, u32[]{:S(2)}) async-start(bf16[4,256,768]{2,1,0:T(8,128)(2,1)} %fusion.35), calls=%async_computation.2 | async-start | bytes 3145728 | tf_op jit(solution)/shard_map/all_to_all | solution.py:97
  256.3 40.9 %all-to-all-start.3 = ((bf16[4,256,768]{2,1,0:T(8,128)(2,1)}), bf16[4,256,768]{2,1,0:T(8,128)(2,1)}, u32[]{:S(2)}, u32[]{:S(2)}) async-start(bf16[4,256,768]{2,1,0:T(8,128)(2,1)} %fusion.32), calls=%async_computation.4 | async-start | bytes 3145728 | tf_op jit(solution)/shard_map/all_to_all | solution.py:126
  260.7 72.7 %all-gather.6.cloned.1.call-start = ((), (), s32[]{:S(2)}) async-start(), calls=%async_computation.8 | async-start | bytes 2359296 | tf_op jit(solution)/shard_map/all_gather | solution.py:133
  305.5 27.8 %copy-start.18 = (bf16[384,768]{1,0:T(8,128)(2,1)S(1)}, bf16[384,768]{1,0:T(8,128)(2,1)}, u32[]{:S(2)}) copy-start(bf16[384,768]{1,0:T(8,128)(2,1)} %param.19) | copy-start | bytes 1769476
  307.8 211.5 %all-reduce.6.cloned.1.call-start = ((), (), s32[]{:S(2)}) async-start(), calls=%async_computation.10 | async-start | bytes 9437184 | tf_op jit(solution)/shard_map/psum | solution.py:181
  335.6 11.3 %copy-start.13 = (bf16[1,1024,384]{1,2,0:T(8,128)(2,1)S(1)}, bf16[1,1024,384]{1,2,0:T(8,128)(2,1)}, u32[]{:S(2)}) copy-start(bf16[1,1024,384]{1,2,0:T(8,128)(2,1)} %copy-done.12) | copy-start | bytes 2359300
  389.4 3.9 copy-start.8
  394.5 3.6 copy-start.15
  394.5 3.6 copy-start.29
  402.0 162.7 %reduce-scatter.5.cloned.1.call-start = ((), (), s32[]{:S(2)}) async-start(), calls=%async_computation.9 | async-start | bytes 4718592 | tf_op jit(solution)/shard_map/reduce_scatter | solution.py:169
  407.2 402.8 %all-reduce.8.cloned.1.call-start = ((), (), s32[]{:S(2)}) async-start(), calls=%async_computation.11 | async-start | bytes 37748736 | tf_op jit(solution)/shard_map/psum | solution.py:16
  519.4 45.4 %copy-start.2 = (bf16[512,768]{1,0:T(8,128)(2,1)S(1)}, bf16[512,768]{1,0:T(8,128)(2,1)}, u32[]{:S(2)}) copy-start(bf16[512,768]{1,0:T(8,128)(2,1)} %param.11) | copy-start | bytes 2359300
  519.4 45.4 %copy-start.20 = (f32[512]{0:T(512)S(1)}, f32[512]{0:T(512)}, u32[]{:S(2)}) copy-start(f32[512]{0:T(512)} %copy-done.19) | copy-start | bytes 6148
  519.4 45.4 %copy-start.21 = (f32[768]{0:T(1024)S(1)}, f32[768]{0:T(1024)}, u32[]{:S(2)}) copy-start(f32[768]{0:T(1024)} %param.16) | copy-start | bytes 9220
  524.6 42.1 %copy-start.26 = (f32[512]{0:T(512)S(1)}, f32[512]{0:T(512)}, u32[]{:S(2)}) copy-start(f32[512]{0:T(512)} %copy-done.25) | copy-start | bytes 6148
  524.6 42.1 %copy-start.24 = (f32[512]{0:T(512)S(1)}, f32[512]{0:T(512)}, u32[]{:S(2)}) copy-start(f32[512]{0:T(512)} %copy-done.23) | copy-start | bytes 6148
  524.6 83.1 %copy-start.10 = (bf16[512,768]{1,0:T(8,128)(2,1)S(1)}, bf16[512,768]{1,0:T(8,128)(2,1)}, u32[]{:S(2)}) copy-start(bf16[512,768]{1,0:T(8,128)(2,1)} %param.12) | copy-start | bytes 2359300
  810.0 11.3 %slice-start = ((s8[9437184]{0:T(1024)(128)(4,1)}), s8[4194304]{0:T(1024)(128)(4,1)S(1)}, s32[]{:S(2)}) async-start(s8[9437184]{0:T(1024)(128)(4,1)} %bitcast.103), calls=%async_computation.12 | async-start | bytes 8388608
  812.5 8.8 %slice-start.1 = ((s8[9437184]{0:T(1024)(128)(4,1)}), s8[4194304]{0:T(1024)(128)(4,1)S(1)}, s32[]{:S(2)}) async-start(s8[9437184]{0:T(1024)(128)(4,1)} %bitcast.103), calls=%async_computation.13 | async-start | bytes 8388608
  812.5 8.8 %slice-start.2 = ((s8[9437184]{0:T(1024)(128)(4,1)}), s8[1048576]{0:T(1024)(128)(4,1)S(1)}, s32[]{:S(2)}) async-start(s8[9437184]{0:T(1024)(128)(4,1)} %bitcast.103), calls=%async_computation.14 | async-start | bytes 2097152
  (13 other events, 21.8 us)
Sparse Core Ops, SparseCore 0:
  13.8 29.8 all-gather.3
  82.7 43.3 reduce-scatter.2
  308.0 25.3 all-gather.5
  402.1 117.1 all-reduce.5
  521.5 43.1 reduce-scatter.4
  569.2 240.7 all-reduce.7
where the time goes:
time: 837 us; the launch traced here: 832 us
  waiting for transfers between devices  503 us (60%)
  matrix products  144 us (17%)
  local copies, waits for them, and re-layouts  53.7 us (6%)
  other arithmetic  51.8 us (6%)
  blocking collectives  45.4 us (5%)
  starting transfers between devices  18.8 us (2%)
  between operations  14.7 us (2%)
    psum x1, waiting for transfers between devices, sum_experts(): return lax.psum((inner_part, outer_part), ('dp', 'head'))  198 us
    psum x1, waiting for transfers between devices, on_device(): lax.psum((project_part, weight_run), ('dp', 'expert'))  89 us
    reduce_scatter x1, waiting for transfers between devices, on_device(): lax.psum_scatter(jnp.einsum('cte,cde->td', mixed_grad, project_weight, pr...  40.2 us
    psum x1, blocking collectives, on_device(): lax.psum((first_gain_part, second_gain_part), ('dp', 'expert', 'head'))  40.1 us
    reduce_scatter x1, waiting for transfers between devices, on_device(): lax.psum_scatter(jnp.dot(row_block, output_weight, preferred_element_type...  37.8 us
    all_to_all x1, waiting for transfers between devices, on_device(): lax.all_to_all(outgoing, 'expert', split_axis=0, concat_axis=0, tiled=True)  32.7 us
    all_to_all x1, waiting for transfers between devices, on_device(): lax.all_to_all(rows_grad, 'expert', split_axis=0, concat_axis=0, tiled=True)  31.8 us
    unnamed x74, local copies, waits for them, and re-layouts  31.4 us
  transfers between devices with their start and end apart: 10, of which 10 were waited for; matrix products, arithmetic and copies ran while one was open for 12% of the time, Pallas kernels for 0%

commit v1 on v0

v1 whole, which is shorter than its diff:
```python
import jax
import jax.numpy as jnp
from jax import lax
from jax.sharding import PartitionSpec as P

HEAD_DIM = 64
BF = jnp.bfloat16
F32 = jnp.float32


def layer_norm(values, gain):
    center = values - jnp.mean(values, axis=-1, keepdims=True)
    spread = jnp.mean(center * center, axis=-1, keepdims=True)
    return center * lax.rsqrt(spread + 1e-05) * gain


def swap(values, axis, bit):
    size = lax.axis_size(axis)
    return lax.ppermute(values, axis, [(i, i ^ bit) for i in range(size)])


def bits_of(axis, low=1):
    size = lax.axis_size(axis)
    found = []
    while low < size:
        found.append((axis, low))
        low *= 2
    return found


def side(axis, bit):
    return (lax.axis_index(axis) // bit) % 2


def half_of(values, which):
    rows = values.shape[0] // 2
    return lax.dynamic_slice_in_dim(values, which * rows, rows, 0)


def scatter_sum(values, steps):
    for axis, bit in steps:
        mine = side(axis, bit)
        got = swap(half_of(values, 1 - mine), axis, bit)
        values = (half_of(values, mine).astype(F32) + got.astype(F32)).astype(BF)
    return values


def gather_back(values, steps):
    for axis, bit in reversed(steps):
        mine = side(axis, bit)
        got = swap(values, axis, bit)
        rows = values.shape[0]
        whole = jnp.zeros((2 * rows,) + values.shape[1:], values.dtype)
        whole = lax.dynamic_update_slice_in_dim(whole, values, mine * rows, 0)
        values = lax.dynamic_update_slice_in_dim(whole, got, (1 - mine) * rows, 0)
    return values


def on_device(
    block_input,
    output_cotangent,
    token_ids,
    positions,
    hash_table,
    first_gain,
    second_gain,
    project_weight,
    output_weight,
    expert_inner,
    expert_outer,
):
    tok_rows, model_width = block_input.shape
    local_cols = output_weight.shape[0]
    head_count = local_cols // HEAD_DIM
    expert_count = lax.axis_size("expert")
    capacity = tok_rows // 2
    inner_weight = expert_inner[0]
    outer_weight = expert_outer[0]
    my_head = lax.axis_index("head")
    my_expert = lax.axis_index("expert")

    chosen = jnp.take(hash_table, token_ids)
    relative = chosen ^ my_expert
    one_hot = relative[:, None] == jnp.arange(expert_count, dtype=jnp.int32)[None, :]
    rank_table = jnp.cumsum(one_hot.astype(jnp.int32), axis=0) - 1
    slot_index = relative * capacity + jnp.sum(jnp.where(one_hot, rank_table, 0), axis=1)
    place = (
        slot_index[None, :] == jnp.arange(expert_count * capacity, dtype=jnp.int32)[:, None]
    ).astype(BF)

    def dispatch(rows):
        return jnp.dot(place, rows, preferred_element_type=F32).astype(BF)

    def exchange(rows):
        blocks = rows.reshape(expert_count, capacity, model_width)
        return [blocks[0]] + [swap(blocks[k], "expert", k) for k in range(1, expert_count)]

    def put_back(blocks):
        return lax.dot_general(
            place,
            jnp.concatenate(blocks, axis=0),
            (((0,), (0,)), ((), ())),
            preferred_element_type=F32,
        )

    grad_blocks = exchange(dispatch(output_cotangent))

    def in_order(own, other):
        return jnp.where(
            my_head == 0,
            jnp.concatenate([own, other], axis=0),
            jnp.concatenate([other, own], axis=0),
        )

    residual = block_input.astype(F32)
    first_low = layer_norm(residual, first_gain).astype(BF)
    gathered = in_order(first_low, swap(first_low, "head", 1))
    seq_pos = in_order(positions, swap(positions, "head", 1))
    seq_len = gathered.shape[0]
    projected = jnp.einsum(
        "td,cde->cte", gathered, project_weight, preferred_element_type=F32
    ).astype(BF)
    head_values = projected.reshape(3, seq_len, head_count, HEAD_DIM)
    ordering = jnp.arange(seq_len, dtype=jnp.int32)
    visible = (ordering[None, :] <= ordering[:, None]) & (
        ordering[None, :] >= (ordering - seq_pos)[:, None]
    )
    scores = (
        jnp.einsum("qhd,khd->hqk", head_values[0], head_values[1], preferred_element_type=F32)
        * 0.125
    )
    scores = jnp.where(visible[None], scores, -1000000000.0)
    row_max = jnp.max(scores, axis=-1, keepdims=True)
    exponent = jnp.exp(scores - row_max)
    row_total = jnp.sum(exponent, axis=-1, keepdims=True)
    log_total = row_max + jnp.log(row_total)
    probabilities = (exponent / row_total).astype(BF)
    context = jnp.einsum(
        "hqk,khd->qhd", probabilities, head_values[2], preferred_element_type=F32
    )
    context = context.astype(BF).reshape(seq_len, local_cols)

    def half_rows(values, which):
        return lax.dynamic_slice_in_dim(values, which * tok_rows, tok_rows, 0)

    theirs = jnp.dot(
        half_rows(context, 1 - my_head), output_weight, preferred_element_type=F32
    ).astype(BF)
    theirs = swap(theirs, "head", 1)
    hidden = (
        residual
        + jnp.dot(half_rows(context, my_head), output_weight, preferred_element_type=F32)
        + theirs.astype(F32)
    )
    second_low = layer_norm(hidden, second_gain).astype(BF)

    row_blocks = exchange(dispatch(second_low))
    arrived = jnp.concatenate(row_blocks, axis=0)
    grad_arrived = jnp.concatenate(grad_blocks, axis=0)
    pre_act = jnp.dot(arrived, inner_weight, preferred_element_type=F32)
    act_grad = lax.dot_general(
        grad_arrived, outer_weight, (((1,), (1,)), ((), ())), preferred_element_type=F32
    )
    pre_grad = jax.vjp(jax.nn.gelu, pre_act)[1](act_grad)[0].astype(BF)
    rows_grad = lax.dot_general(
        pre_grad, inner_weight, (((1,), (1,)), ((), ())), preferred_element_type=F32
    ).astype(BF)
    returned = exchange(rows_grad)
    activated = jax.nn.gelu(pre_act).astype(BF)
    produced = jnp.dot(activated, outer_weight, preferred_element_type=F32).astype(BF)
    combined = exchange(produced)
    block_output = (hidden + put_back(combined)).astype(BF)

    core = side("dp", 1)

    def halves_sum(left, right):
        def part(which):
            cols = left.shape[1] // 2
            return lax.dot_general(
                lax.dynamic_slice_in_dim(left, which * cols, cols, 1),
                right,
                (((0,), (0,)), ((), ())),
                preferred_element_type=F32,
            )

        got = swap(part(1 - core).astype(BF), "dp", 1)
        return (part(core) + got.astype(F32)).astype(BF)

    steps = bits_of("dp", 2) + bits_of("head")
    outer_part = scatter_sum(halves_sum(activated, grad_arrived), steps)
    inner_part = scatter_sum(halves_sum(arrived, pre_grad), steps[::-1])
    outer_total = gather_back(gather_back(outer_part, steps), [("dp", 1)]).astype(F32)
    inner_total = gather_back(gather_back(inner_part, steps[::-1]), [("dp", 1)]).astype(F32)

    second_grad = put_back(returned)
    second_back = jax.vjp(layer_norm, hidden, second_gain)[1]
    hidden_part, second_gain_part = second_back(second_grad)
    hidden_grad = output_cotangent.astype(F32) + hidden_part

    hidden_low = hidden_grad.astype(BF)
    shard_rows = in_order(hidden_low, swap(hidden_low, "head", 1))
    context_grad = jnp.einsum("td,cd->tc", shard_rows, output_weight, preferred_element_type=F32)
    weight_run = jnp.einsum("tc,td->cd", context, shard_rows, preferred_element_type=F32)
    context_grad = context_grad.astype(BF).reshape(seq_len, head_count, HEAD_DIM)
    scores = (
        jnp.einsum("qhd,khd->hqk", head_values[0], head_values[1], preferred_element_type=F32)
        * 0.125
    )
    scores = jnp.where(visible[None], scores, -1000000000.0)
    soft = jnp.exp(scores - log_total)
    value_grad = jnp.einsum(
        "hqk,qhd->khd", soft.astype(BF), context_grad, preferred_element_type=F32
    ).astype(BF)
    prob_grad = jnp.einsum(
        "qhd,khd->hqk", context_grad, head_values[2], preferred_element_type=F32
    )
    inner_sum = jnp.sum(soft * prob_grad, axis=-1, keepdims=True)
    score_grad = (soft * (prob_grad - inner_sum)).astype(BF)
    query_grad = (
        jnp.einsum("hqk,khd->qhd", score_grad, head_values[1], preferred_element_type=F32) * 0.125
    ).astype(BF)
    key_grad = (
        jnp.einsum("hqk,qhd->khd", score_grad, head_values[0], preferred_element_type=F32) * 0.125
    ).astype(BF)
    mixed_grad = jnp.stack([query_grad, key_grad, value_grad]).reshape(3, seq_len, local_cols)
    project_part = jnp.einsum("td,cte->cde", gathered, mixed_grad, preferred_element_type=F32)

    def first_rows(which):
        return jnp.einsum(
            "cte,cde->td",
            lax.dynamic_slice_in_dim(mixed_grad, which * tok_rows, tok_rows, 1),
            project_weight,
            preferred_element_type=F32,
        )

    theirs = swap(first_rows(1 - my_head).astype(BF), "head", 1)
    first_grad = first_rows(my_head) + theirs.astype(F32)
    input_part, _ = jax.vjp(layer_norm, residual, first_gain)[1](first_grad)
    input_grad = hidden_grad + input_part

    first_gain_part = (
        jnp.sum(project_part * project_weight.astype(F32), axis=(0, 2)) / first_gain
    )
    gains = jnp.stack([first_gain_part, second_gain_part])
    for axis, bit in bits_of("dp") + bits_of("expert") + bits_of("head"):
        gains = gains + swap(gains, axis, bit)

    steps = bits_of("dp") + bits_of("expert")
    project_part = project_part.reshape(3 * model_width, local_cols).astype(BF)
    project_grad = gather_back(scatter_sum(project_part, steps), steps).astype(F32)
    output_weight_grad = gather_back(scatter_sum(weight_run.astype(BF), steps), steps).astype(F32)
    return (
        block_output,
        input_grad,
        gains[0],
        gains[1],
        project_grad.reshape(3, model_width, local_cols),
        output_weight_grad,
        inner_total[None],
        outer_total[None],
    )


def solution(mesh):
    in_specs = (
        P(("dp", "expert", "head"), None),
        P(("dp", "expert", "head"), None),
        P(("dp", "expert", "head")),
        P(("dp", "expert", "head")),
        P(),
        P(),
        P(),
        P(None, None, "head"),
        P("head", None),
        P("expert", None, None),
        P("expert", None, None),
    )
    out_specs = (
        P(("dp", "expert", "head"), None),
        P(("dp", "expert", "head"), None),
        P(),
        P(),
        P(None, None, "head"),
        P("head", None),
        P("expert", None, None),
        P("expert", None, None),
    )
    return jax.shard_map(
        on_device, mesh=mesh, in_specs=in_specs, out_specs=out_specs, check_vma=False
    )
```

time: 837 us -> 501 us (0.60)
  waiting for transfers between devices: 503 us -> 177 us
  starting transfers between devices: 18.8 us -> 83.8 us
  blocking collectives: 45.4 us -> 0 us
  local copies, waits for them, and re-layouts: 53.7 us -> 26.5 us
  between operations: 14.7 us -> 2.28 us
    psum x2 -> x0, waiting for transfers between devices: 288 us -> none  [the longest x1 198 us: sum_experts(): return lax.psum((inner_part, outer_part), ('dp', 'head'))]
    ppermute x0 -> x50, waiting for transfers between devices: none -> 177 us  [swap(): return lax.ppermute(values, axis, [(i, i ^ bit) for i in range(size)])]
    all_to_all x4 -> x0, waiting for transfers between devices: 88.3 us -> none  [the longest x1 32.7 us: on_device(): lax.all_to_all(outgoing, 'expert', split_axis=0, concat_axis=0, tiled=True)]
    ppermute x0 -> x50, starting transfers between devices: none -> 83.8 us  [swap(): return lax.ppermute(values, axis, [(i, i ^ bit) for i in range(size)])]
    reduce_scatter x2 -> x0, waiting for transfers between devices: 78 us -> none  [the longest x1 40.2 us: on_device(): lax.psum_scatter(jnp.einsum('cte,cde->td', mixed_grad, project_weight, pr...]
    all_gather x2 -> x0, waiting for transfers between devices: 49.4 us -> none  [the longest x1 25.3 us: on_device(): lax.all_gather(hidden_grad.astype(jnp.bfloat16), 'head', axis=0, tiled=True)]
    psum x1 -> x0, blocking collectives: 40.1 us -> none  [on_device(): lax.psum((first_gain_part, second_gain_part), ('dp', 'expert', 'head'))]
    unnamed x74 -> x101, local copies, waits for them, and re-layouts: 31.4 us -> 6.59 us
  transfers between devices with their start and end apart: 10 -> 50, of which waited for: 10 -> 22; matrix products, arithmetic and copies ran while one was open for 12% -> 31% of each run, Pallas kernels for 0% -> 0%
where the time goes in v1:
time: 501 us; the launch traced here: 494 us
  waiting for transfers between devices  177 us (35%)
  matrix products  151 us (30%)
  starting transfers between devices  83.8 us (17%)
  other arithmetic  53.2 us (11%)
  local copies, waits for them, and re-layouts  26.5 us (5%)
    ppermute x50, waiting for transfers between devices, swap(): return lax.ppermute(values, axis, [(i, i ^ bit) for i in range(size)])  177 us
    ppermute x50, starting transfers between devices, swap(): return lax.ppermute(values, axis, [(i, i ^ bit) for i in range(size)])  83.8 us
    dot_general x4, matrix products, part(): lax.dot_general(lax.dynamic_slice_in_dim(left, which * cols, cols, 1), ri...  18.8 us
    convert_element_type x1, other arithmetic, on_device(): score_grad = (soft * (prob_grad - inner_sum)).astype(BF)  16.8 us
    dot_general x1, matrix products, on_device(): lax.dot_general(grad_arrived, outer_weight, (((1,), (1,)), ((), ())), pre...  16.3 us
    dot_general x1, matrix products, on_device(): jnp.einsum('qhd,khd->hqk', context_grad, head_values[2], preferred_elemen...  16 us
    dot_general x1, matrix products, on_device(): pre_act = jnp.dot(arrived, inner_weight, preferred_element_type=F32)  13.6 us
    dot_general x1, matrix products, on_device(): jnp.einsum('hqk,qhd->khd', soft.astype(BF), context_grad, preferred_eleme...  11.2 us
  transfers between devices with their start and end apart: 50, of which 22 were waited for; matrix products, arithmetic and copies ran while one was open for 31% of the time, Pallas kernels for 0%

profile of v1, /device:TPU:0, one launch (start us, length us, event | category | flops | bytes accessed | tf_op | source)
XLA Modules:
  0.0 493.5 jit_solution(2587968898340996471)
XLA Ops:
  13.7 12.7 %collective-permute-done.1 = s32[512]{0:T(512)S(1)} collective-permute-done((s32[512]{0:T(512)S(1)}, s32[512]{0:T(512)S(1)}, u32[]{:S(2)}, u32[]{:S(2)}) %collective-permute-start.1) | collective-permute-done | bytes 2080 | tf_op jit(solution)/shard_map/ppermute | solution.py:19
  30.8 10.7 %fusion.115 = (f32[6,1024]{1,0:T(8,128)S(1)}, f32[6,1024,1024]{1,2,0:T(8,128)}) fusion(bf16[1024,6,64]{0,2,1:T(8,128)(2,1)S(1)} %bitcast.105, bf16[1024,6,64]{0,2,1:T(8,128)(2,1)S(1)} %bitcast.103, pred[1024,1024]{0,1:T(8,128)(4,1)S(1)} %fusion.21), kind=kOutput, calls=%fused_computation.220 | convolution fusion | flops 824174592 | bytes 27811840 | tf_op jit(solution)/shard_map/qhd,khd->hqk/dot_general | solution.py:129
  41.5 10.2 %fusion = f32[6,1024]{1,0:T(8,128)S(1)} fusion(f32[6,1024,1024]{1,2,0:T(8,128)} %get-tuple-element.42, f32[6,1024]{1,0:T(8,128)S(1)} %get-tuple-element.41), kind=kLoop, calls=%fused_computation.7 | loop fusion | flops 12576768 | bytes 25214976 | tf_op jit(solution)/shard_map/reduce_sum | solution.py:135
  51.7 10.8 %fusion.69 = bf16[6,64,1024]{2,1,0:T(8,128)(2,1)S(1)} fusion(bf16[1024,6,64]{0,2,1:T(8,128)(2,1)S(1)} %bitcast.117, f32[6,1024,1024]{1,2,0:T(8,128)} %get-tuple-element.42, f32[6,1024]{1,0:T(8,128)S(1)} %fusion, f32[6,1024]{1,0:T(8,128)S(1)} %get-tuple-element.41), kind=kOutput, calls=%fused_computation.108 | convolution fusion | flops 824573952 | bytes 26787840 | tf_op jit(solution)/shard_map/hqk,khd->qhd/dot_general | solution.py:138
  66.1 15.8 %collective-permute-done.2 = bf16[512,768]{1,0:T(8,128)(2,1)S(1)} collective-permute-done((bf16[512,768]{1,0:T(8,128)(2,1)S(1)}, bf16[512,768]{1,0:T(8,128)(2,1)S(1)}, u32[]{:S(2)}, u32[]{:S(2)}) %collective-permute-start.2) | collective-permute-done | bytes 786464 | tf_op jit(solution)/shard_map/ppermute | solution.py:19
  99.6 17.4 %collective-permute-start.9 = (bf16[256,768]{1,0:T(8,128)(2,1)}, bf16[256,768]{1,0:T(8,128)(2,1)S(1)}, u32[]{:S(2)}, u32[]{:S(2)}) collective-permute-start(bf16[256,768]{1,0:T(8,128)(2,1)} %get-tuple-element.32), channel_id=1, source_target_pairs={{0,2},{2,0},{4,6},{6,4},{1,3},{3,1},{5,7},{7,5},{8,10},{10,8},{12,... | collective-permute-start | bytes 1179656 | tf_op jit(solution)/shard_map/ppermute | solution.py:19
  117.0 22.1 %collective-permute-done.4 = bf16[256,768]{1,0:T(8,128)(2,1)} collective-permute-done((bf16[256,768]{1,0:T(8,128)(2,1)}, bf16[256,768]{1,0:T(8,128)(2,1)}, u32[]{:S(2)}, u32[]{:S(2)}) %collective-permute-start.4) | collective-permute-done | bytes 393248 | tf_op jit(solution)/shard_map/ppermute | solution.py:19
  139.1 13.6 %multiply_convert_fusion.1 = (bf16[1024,3072]{1,0:T(8,128)(2,1)S(1)}, f32[1024,3072]{1,0:T(8,128)}) fusion(bf16[1,768,3072]{2,1,0:T(8,128)(2,1)} %param.20, bf16[256,768]{1,0:T(8,128)(2,1)} %collective-permute-done.5, bf16[256,768]{1,0:T(8,128)(2,1)} %collective-permute-done.4, bf16[256,768]{1,0:T(8,128)(2,1)} %collective-permute-done.3, ...), kind=kOutput, calls=%fused_computation.20 | convolution fusion | flops 4866441216 | bytes 25165824 | tf_op jit(solution)/shard_map/dot_general | solution.py:160
  152.8 9.6 %fusion.40 = bf16[1024,768]{1,0:T(8,128)(2,1)S(1)} fusion(bf16[1024,3072]{1,0:T(8,128)(2,1)S(1)} %get-tuple-element.45, bf16[1,3072,768]{2,1,0:T(8,128)(2,1)} %param.21), kind=kOutput, calls=%fused_computation.68 | convolution fusion | flops 4832624640 | bytes 12582912 | tf_op jit(solution)/shard_map/dot_general | solution.py:170
  163.2 16.3 %fusion.8 = bf16[1024,3072]{1,0:T(8,128)(2,1)S(1)} fusion(f32[1024,3072]{1,0:T(8,128)} %get-tuple-element.46, bf16[1,3072,768]{2,1,0:T(8,128)(2,1)} %param.21, bf16[256,768]{1,0:T(8,128)(2,1)} %collective-permute-done.11, bf16[256,768]{1,0:T(8,128)(2,1)} %collective-permute-done.10, bf16[256,768]{1,0:T(8,128)(2,1)} %copy-done.42, ...), kind=kOutput, calls=%fused_computation.17 | convolution fusion | flops 4901044224 | bytes 25165824 | tf_op jit(solution)/shard_map/dot_general | solution.py:161
  179.5 9.7 %fusion.37 = bf16[1024,768]{1,0:T(8,128)(2,1)S(1)} fusion(bf16[1024,3072]{1,0:T(8,128)(2,1)S(1)} %fusion.8, bf16[1,768,3072]{2,1,0:T(8,128)(2,1)} %param.20), kind=kOutput, calls=%fused_computation.67 | convolution fusion | flops 4832624640 | bytes 12582912 | tf_op jit(solution)/shard_map/dot_general | solution.py:165
  203.3 17.4 %collective-permute-start.6 = (bf16[256,768]{1,0:T(8,128)(2,1)}, bf16[256,768]{1,0:T(8,128)(2,1)}, u32[]{:S(2)}, u32[]{:S(2)}) collective-permute-start(bf16[256,768]{1,0:T(8,128)(2,1)} %get-tuple-element.36), channel_id=1, source_target_pairs={{0,2},{2,0},{4,6},{6,4},{1,3},{3,1},{5,7},{7,5},{8,10},{10,8},{12,... | collective-permute-start | bytes 1179656 | tf_op jit(solution)/shard_map/ppermute | solution.py:19
  220.7 21.2 %collective-permute-done.13 = bf16[256,768]{1,0:T(8,128)(2,1)S(1)} collective-permute-done((bf16[256,768]{1,0:T(8,128)(2,1)S(1)}, bf16[256,768]{1,0:T(8,128)(2,1)S(1)}, u32[]{:S(2)}, u32[]{:S(2)}) %collective-permute-start.13) | collective-permute-done | bytes 393248 | tf_op jit(solution)/shard_map/ppermute | solution.py:19
  251.5 5.1 %convolution_convert_fusion.1 = bf16[1536,768]{1,0:T(8,128)(2,1)} fusion(bf16[1024,3072]{1,0:T(8,128)(2,1)S(1)} %bitcast.126, s32[]{:T(128)S(6)} %select_n.300, bf16[256,768]{1,0:T(8,128)(2,1)} %collective-permute-done.11, bf16[256,768]{1,0:T(8,128)(2,1)} %collective-permute-done.10, bf16[256,768]{1,0:T(8,128)(2,1)S(1)} %copy-done.43, ...), kind=kOutput, calls=%fused_computation.39 | convolution fusion | flops 2423390208 | bytes 7077892 | tf_op jit(solution)/shard_map/dot_general | solution.py:179
  258.5 11.2 %fusion.66 = bf16[6,64,1024]{2,1,0:T(8,128)(2,1)} fusion(bf16[1024,6,64]{0,2,1:T(8,128)(2,1)S(1)} %bitcast.113, f32[6,1024,1024]{1,2,0:T(8,128)} %get-tuple-element.42, f32[6,1024]{1,0:T(8,128)S(1)} %log_add_fusion), kind=kOutput, calls=%fused_computation.106 | convolution fusion | flops 818282496 | bytes 26763264 | tf_op jit(solution)/shard_map/hqk,qhd->khd/dot_general | solution.py:211
  269.7 16.0 %multiply_reduce_fusion = (f32[6,1024]{1,0:T(8,128)S(1)}, f32[6,1024,1024]{1,2,0:T(8,128)}) fusion(f32[6,1024,1024]{1,2,0:T(8,128)} %get-tuple-element.42, f32[6,1024]{1,0:T(8,128)S(1)} %log_add_fusion, bf16[1024,6,64]{0,2,1:T(8,128)(2,1)S(1)} %bitcast.114, bf16[1024,6,64]{0,2,1:T(8,128)(2,1)S(1)} %bitcast.118), kind=kOutput, calls=%fused_computation.2 | convolution fusion | flops 824174592 | bytes 51953664 | tf_op jit(solution)/shard_map/qhd,khd->hqk/dot_general | solution.py:214
  285.8 16.8 %multiply_convert_fusion = bf16[6,1024,1024]{1,2,0:T(8,128)(2,1)S(1)} fusion(f32[6,1024,1024]{1,2,0:T(8,128)} %get-tuple-element.49, f32[6,1024,1024]{1,2,0:T(8,128)} %get-tuple-element.42, f32[6,1024]{1,0:T(8,128)S(1)} %get-tuple-element.48, f32[6,1024]{1,0:T(8,128)S(1)} %log_add_fusion), kind=kLoop, calls=%fused_computation.1 | loop fusion | flops 25165824 | bytes 62963712 | tf_op jit(solution)/shard_map/convert_element_type | solution.py:218
  302.6 6.1 %multiply_convert_fusion.2 = bf16[6,64,1024]{2,1,0:T(8,128)(2,1)} fusion(bf16[1024,6,64]{0,2,1:T(8,128)(2,1)} %bitcast.106, bf16[6,1024,1024]{1,2,0:T(8,128)(2,1)S(1)} %multiply_convert_fusion), kind=kOutput, calls=%fused_computation.98 | convolution fusion | flops 806092800 | bytes 14155776 | tf_op jit(solution)/shard_map/hqk,qhd->khd/dot_general | solution.py:223
  316.4 6.0 %fusion.24 = (f32[768]{0:T(1024)S(1)}, bf16[3,384,768]{2,1,0:T(8,128)(2,1)}) fusion(bf16[3,768,384]{1,2,0:T(8,128)(2,1)} %copy.38, bf16[512,768]{1,0:T(8,128)(2,1)} %collective-permute-done, bf16[512,768]{1,0:T(8,128)(2,1)} %copy-done.23, pred[]{:T(512)S(6)} %eq.69, bf16[1,1024,384]{2,1,0:T(8,128)(2,1)S(1)} %copy.36, bf16[1,1024,384]{2,1,0:T(8,128)(2,1)S(1)} %copy.35, ...), kind=kOutput, calls=%fused_computation.38 | convolution fusion | flops 1824914688 | bytes 7474177 | tf_op jit(solution)/shard_map/td,cte->cde/dot_general | solution.py:226
  345.1 12.8 %collective-permute-done.21 = f32[2,768]{1,0:T(2,128)S(1)} collective-permute-done((f32[2,768]{1,0:T(2,128)S(1)}, f32[2,768]{1,0:T(2,128)S(1)}, u32[]{:S(2)}, u32[]{:S(2)}) %collective-permute-start.21) | collective-permute-done | bytes 6176 | tf_op jit(solution)/shard_map/ppermute | solution.py:19
  359.2 4.4 collective-permute-done.34
  363.7 4.3 collective-permute-done.35
  383.6 5.5 %add_convert_fusion = bf16[1536,768]{1,0:T(8,128)(2,1)S(1)} fusion(bf16[1536,768]{1,0:T(8,128)(2,1)} %collective-permute-done.44, bf16[1024,3072]{1,0:T(8,128)(2,1)} %copy-done.45, s32[]{:T(128)S(6)} %select_n.299, bf16[256,768]{1,0:T(8,128)(2,1)} %collective-permute-done.11, bf16[256,768]{1,0:T(8,128)(2,1)} %collective-permute-done.10, ...), kind=kOutput, calls=%fused_computation.30 | convolution fusion | flops 2425749504 | bytes 9437188 | tf_op jit(solution)/shard_map/dot_general | solution.py:179
  392.5 5.2 %collective-permute-done.25 = bf16[144,384]{1,0:T(8,128)(2,1)S(1)} collective-permute-done((bf16[144,384]{1,0:T(8,128)(2,1)S(1)}, bf16[144,384]{1,0:T(8,128)(2,1)S(1)}, u32[]{:S(2)}, u32[]{:S(2)}) %collective-permute-start.25) | collective-permute-done | bytes 110624 | tf_op jit(solution)/shard_map/ppermute | solution.py:19
  397.8 6.5 %collective-permute-done.39 = bf16[192,3072]{1,0:T(8,128)(2,1)S(1)} collective-permute-done((bf16[192,3072]{1,0:T(8,128)(2,1)S(1)}, bf16[192,3072]{1,0:T(8,128)(2,1)S(1)}, u32[]{:S(2)}, u32[]{:S(2)}) %collective-permute-start.39) | collective-permute-done | bytes 1179680 | tf_op jit(solution)/shard_map/ppermute | solution.py:19
  407.5 12.2 %collective-permute-done.45 = bf16[768,768]{1,0:T(8,128)(2,1)S(1)} collective-permute-done((bf16[768,768]{1,0:T(8,128)(2,1)S(1)}, bf16[768,768]{1,0:T(8,128)(2,1)S(1)}, u32[]{:S(2)}, u32[]{:S(2)}) %collective-permute-start.45) | collective-permute-done | bytes 1179680 | tf_op jit(solution)/shard_map/ppermute | solution.py:19
  421.6 7.6 %collective-permute-done.40 = bf16[96,3072]{1,0:T(8,128)(2,1)S(1)} collective-permute-done((bf16[96,3072]{1,0:T(8,128)(2,1)S(1)}, bf16[96,3072]{1,0:T(8,128)(2,1)S(1)}, u32[]{:S(2)}, u32[]{:S(2)}) %collective-permute-start.40) | collective-permute-done | bytes 589856 | tf_op jit(solution)/shard_map/ppermute | solution.py:19
  433.6 12.2 %collective-permute-done.41 = bf16[96,3072]{1,0:T(8,128)(2,1)S(1)} collective-permute-done((bf16[96,3072]{1,0:T(8,128)(2,1)S(1)}, bf16[96,3072]{1,0:T(8,128)(2,1)S(1)}, u32[]{:S(2)}, u32[]{:S(2)}) %collective-permute-start.41) | collective-permute-done | bytes 589856 | tf_op jit(solution)/shard_map/ppermute | solution.py:19
  452.8 15.1 %collective-permute-done.42 = bf16[192,3072]{1,0:T(8,128)(2,1)S(1)} collective-permute-done((bf16[192,3072]{1,0:T(8,128)(2,1)S(1)}, bf16[192,3072]{1,0:T(8,128)(2,1)S(1)}, u32[]{:S(2)}, u32[]{:S(2)}) %collective-permute-start.42) | collective-permute-done | bytes 1179680 | tf_op jit(solution)/shard_map/ppermute | solution.py:19
  470.0 9.3 %collective-permute-done.48 = bf16[768,768]{1,0:T(8,128)(2,1)S(1)} collective-permute-done((bf16[768,768]{1,0:T(8,128)(2,1)S(1)}, bf16[768,768]{1,0:T(8,128)(2,1)S(1)}, u32[]{:S(2)}, u32[]{:S(2)}) %collective-permute-start.48) | collective-permute-done | bytes 1179680 | tf_op jit(solution)/shard_map/ppermute | solution.py:19
  483.5 5.1 %broadcast_in_dim.145 = f32[1,768,3072]{2,1,0:T(8,128)} convert(bf16[1,768,3072]{2,1,0:T(8,128)(2,1)S(1)} %bitcast_dynamic-update-slice_fusion.2) | non-fusion elementwise | flops 2359296 | bytes 14155776 | tf_op jit(solution)/shard_map/broadcast_in_dim | solution.py:259
  488.9 4.5 broadcast_in_dim.151
  (316 shorter events, 137.7 us)
Async XLA Ops:
  5.8 21.3 %collective-permute-start = (bf16[512,768]{1,0:T(8,128)(2,1)S(1)}, bf16[512,768]{1,0:T(8,128)(2,1)}, u32[]{:S(2)}, u32[]{:S(2)}) collective-permute-start(bf16[512,768]{1,0:T(8,128)(2,1)S(1)} %fusion.45), channel_id=1, source_target_pairs={{0,1},{1,0},{2,3},{3,2},{4,5},{5,4},{6,7},{7,6},{8,9},{9,8},{10,11... | collective-permute-start | bytes 2359304 | tf_op jit(solution)/shard_map/ppermute | solution.py:19
  8.8 17.7 %collective-permute-start.1 = (s32[512]{0:T(512)S(1)}, s32[512]{0:T(512)S(1)}, u32[]{:S(2)}, u32[]{:S(2)}) collective-permute-start(s32[512]{0:T(512)S(1)} %copy-done.39), channel_id=1, source_target_pairs={{0,1},{1,0},{2,3},{3,2},{4,5},{5,4},{6,7},{7,6},{8,9},{9,8},{10,11... | collective-permute-start | bytes 6152 | tf_op jit(solution)/shard_map/ppermute | solution.py:19
  63.1 18.8 %collective-permute-start.2 = (bf16[512,768]{1,0:T(8,128)(2,1)S(1)}, bf16[512,768]{1,0:T(8,128)(2,1)S(1)}, u32[]{:S(2)}, u32[]{:S(2)}) collective-permute-start(bf16[512,768]{1,0:T(8,128)(2,1)S(1)} %convolution_convert_fusion.3), channel_id=1, source_target_pairs={{0,1},{1,0},{2,3},{3,2},{4,5},{5,4},{6,7},{7,6},{8,9},{9,8},{10,11... | collective-permute-start | bytes 2359304 | tf_op jit(solution)/shard_map/ppermute | solution.py:19
  85.3 14.3 %collective-permute-start.5 = (bf16[256,768]{1,0:T(8,128)(2,1)}, bf16[256,768]{1,0:T(8,128)(2,1)}, u32[]{:S(2)}, u32[]{:S(2)}) collective-permute-start(bf16[256,768]{1,0:T(8,128)(2,1)} %get-tuple-element.38), channel_id=1, source_target_pairs={{0,6},{2,4},{4,2},{6,0},{1,7},{3,5},{5,3},{7,1},{8,14},{10,12},{12... | collective-permute-start | bytes 1179656 | tf_op jit(solution)/shard_map/ppermute | solution.py:19
  88.8 50.3 %collective-permute-start.4 = (bf16[256,768]{1,0:T(8,128)(2,1)}, bf16[256,768]{1,0:T(8,128)(2,1)}, u32[]{:S(2)}, u32[]{:S(2)}) collective-permute-start(bf16[256,768]{1,0:T(8,128)(2,1)} %get-tuple-element.39), channel_id=1, source_target_pairs={{0,4},{2,6},{4,0},{6,2},{1,5},{3,7},{5,1},{7,3},{8,12},{10,14},{12... | collective-permute-start | bytes 1179656 | tf_op jit(solution)/shard_map/ppermute | solution.py:19
  88.8 50.3 %collective-permute-start.3 = (bf16[256,768]{1,0:T(8,128)(2,1)}, bf16[256,768]{1,0:T(8,128)(2,1)}, u32[]{:S(2)}, u32[]{:S(2)}) collective-permute-start(bf16[256,768]{1,0:T(8,128)(2,1)} %get-tuple-element.40), channel_id=1, source_target_pairs={{0,2},{2,0},{4,6},{6,4},{1,3},{3,1},{5,7},{7,5},{8,10},{10,8},{12,... | collective-permute-start | bytes 1179656 | tf_op jit(solution)/shard_map/ppermute | solution.py:19
  90.9 71.5 %collective-permute-start.11 = (bf16[256,768]{1,0:T(8,128)(2,1)}, bf16[256,768]{1,0:T(8,128)(2,1)}, u32[]{:S(2)}, u32[]{:S(2)}) collective-permute-start(bf16[256,768]{1,0:T(8,128)(2,1)} %get-tuple-element.30), channel_id=1, source_target_pairs={{0,6},{2,4},{4,2},{6,0},{1,7},{3,5},{5,3},{7,1},{8,14},{10,12},{12... | collective-permute-start | bytes 1179656 | tf_op jit(solution)/shard_map/ppermute | solution.py:19
  94.4 68.0 %collective-permute-start.10 = (bf16[256,768]{1,0:T(8,128)(2,1)}, bf16[256,768]{1,0:T(8,128)(2,1)}, u32[]{:S(2)}, u32[]{:S(2)}) collective-permute-start(bf16[256,768]{1,0:T(8,128)(2,1)} %get-tuple-element.31), channel_id=1, source_target_pairs={{0,4},{2,6},{4,0},{6,2},{1,5},{3,7},{5,1},{7,3},{8,12},{10,14},{12... | collective-permute-start | bytes 1179656 | tf_op jit(solution)/shard_map/ppermute | solution.py:19
  99.6 62.9 %collective-permute-start.9 = (bf16[256,768]{1,0:T(8,128)(2,1)}, bf16[256,768]{1,0:T(8,128)(2,1)S(1)}, u32[]{:S(2)}, u32[]{:S(2)}) collective-permute-start(bf16[256,768]{1,0:T(8,128)(2,1)} %get-tuple-element.32), channel_id=1, source_target_pairs={{0,2},{2,0},{4,6},{6,4},{1,3},{3,1},{5,7},{7,5},{8,10},{10,8},{12,... | collective-permute-start | bytes 1179656 | tf_op jit(solution)/shard_map/ppermute | solution.py:19
  189.3 14.0 %collective-permute-start.14 = (bf16[256,768]{1,0:T(8,128)(2,1)S(1)}, bf16[256,768]{1,0:T(8,128)(2,1)S(1)}, u32[]{:S(2)}, u32[]{:S(2)}) collective-permute-start(bf16[256,768]{1,0:T(8,128)(2,1)S(1)} %get-tuple-element.26), channel_id=1, source_target_pairs={{0,6},{2,4},{4,2},{6,0},{1,7},{3,5},{5,3},{7,1},{8,14},{10,12},{12... | collective-permute-start | bytes 1179656 | tf_op jit(solution)/shard_map/ppermute | solution.py:19
  192.6 49.3 %collective-permute-start.13 = (bf16[256,768]{1,0:T(8,128)(2,1)S(1)}, bf16[256,768]{1,0:T(8,128)(2,1)S(1)}, u32[]{:S(2)}, u32[]{:S(2)}) collective-permute-start(bf16[256,768]{1,0:T(8,128)(2,1)S(1)} %get-tuple-element.27), channel_id=1, source_target_pairs={{0,4},{2,6},{4,0},{6,2},{1,5},{3,7},{5,1},{7,3},{8,12},{10,14},{12... | collective-permute-start | bytes 1179656 | tf_op jit(solution)/shard_map/ppermute | solution.py:19
  192.6 49.3 %collective-permute-start.12 = (bf16[256,768]{1,0:T(8,128)(2,1)S(1)}, bf16[256,768]{1,0:T(8,128)(2,1)S(1)}, u32[]{:S(2)}, u32[]{:S(2)}) collective-permute-start(bf16[256,768]{1,0:T(8,128)(2,1)S(1)} %get-tuple-element.28), channel_id=1, source_target_pairs={{0,2},{2,0},{4,6},{6,4},{1,3},{3,1},{5,7},{7,5},{8,10},{10,8},{12,... | collective-permute-start | bytes 1179656 | tf_op jit(solution)/shard_map/ppermute | solution.py:19
  195.0 129.0 %collective-permute-start.8 = (bf16[256,768]{1,0:T(8,128)(2,1)}, bf16[256,768]{1,0:T(8,128)(2,1)}, u32[]{:S(2)}, u32[]{:S(2)}) collective-permute-start(bf16[256,768]{1,0:T(8,128)(2,1)} %get-tuple-element.34), channel_id=1, source_target_pairs={{0,6},{2,4},{4,2},{6,0},{1,7},{3,5},{5,3},{7,1},{8,14},{10,12},{12... | collective-permute-start | bytes 1179656 | tf_op jit(solution)/shard_map/ppermute | solution.py:19
  198.2 126.1 %collective-permute-start.7 = (bf16[256,768]{1,0:T(8,128)(2,1)}, bf16[256,768]{1,0:T(8,128)(2,1)}, u32[]{:S(2)}, u32[]{:S(2)}) collective-permute-start(bf16[256,768]{1,0:T(8,128)(2,1)} %get-tuple-element.35), channel_id=1, source_target_pairs={{0,4},{2,6},{4,0},{6,2},{1,5},{3,7},{5,1},{7,3},{8,12},{10,14},{12... | collective-permute-start | bytes 1179656 | tf_op jit(solution)/shard_map/ppermute | solution.py:19
  203.3 122.8 %collective-permute-start.6 = (bf16[256,768]{1,0:T(8,128)(2,1)}, bf16[256,768]{1,0:T(8,128)(2,1)}, u32[]{:S(2)}, u32[]{:S(2)}) collective-permute-start(bf16[256,768]{1,0:T(8,128)(2,1)} %get-tuple-element.36), channel_id=1, source_target_pairs={{0,2},{2,0},{4,6},{6,4},{1,3},{3,1},{5,7},{7,5},{8,10},{10,8},{12,... | collective-permute-start | bytes 1179656 | tf_op jit(solution)/shard_map/ppermute | solution.py:19
  251.4 122.4 %collective-permute-start.38 = (bf16[384,3072]{1,0:T(8,128)(2,1)}, bf16[384,3072]{1,0:T(8,128)(2,1)}, u32[]{:S(2)}, u32[]{:S(2)}) collective-permute-start(bf16[384,3072]{1,0:T(8,128)(2,1)} %convolution_convert_fusion), channel_id=1, source_target_pairs={{0,8},{8,0},{16,24},{24,16},{1,9},{9,1},{17,25},{25,17},{2,10},{10... | collective-permute-start | bytes 7077896 | tf_op jit(solution)/shard_map/ppermute | solution.py:19
  323.7 59.9 %collective-permute-start.44 = (bf16[1536,768]{1,0:T(8,128)(2,1)}, bf16[1536,768]{1,0:T(8,128)(2,1)}, u32[]{:S(2)}, u32[]{:S(2)}) collective-permute-start(bf16[1536,768]{1,0:T(8,128)(2,1)} %convolution_convert_fusion.1), channel_id=1, source_target_pairs={{0,8},{8,0},{16,24},{24,16},{1,9},{9,1},{17,25},{25,17},{2,10},{10... | collective-permute-start | bytes 7077896 | tf_op jit(solution)/shard_map/ppermute | solution.py:19
  339.5 28.6 %collective-permute-start.16 = (bf16[512,768]{1,0:T(8,128)(2,1)}, bf16[512,768]{1,0:T(8,128)(2,1)}, u32[]{:S(2)}, u32[]{:S(2)}) collective-permute-start(bf16[512,768]{1,0:T(8,128)(2,1)} %bitcast_convert_fusion.1), channel_id=1, source_target_pairs={{0,1},{1,0},{2,3},{3,2},{4,5},{5,4},{6,7},{7,6},{8,9},{9,8},{10,11... | collective-permute-start | bytes 2359304 | tf_op jit(solution)/shard_map/ppermute | solution.py:19
  344.0 13.9 %collective-permute-start.21 = (f32[2,768]{1,0:T(2,128)S(1)}, f32[2,768]{1,0:T(2,128)S(1)}, u32[]{:S(2)}, u32[]{:S(2)}) collective-permute-start(f32[2,768]{1,0:T(2,128)S(1)} %add.308), channel_id=1, source_target_pairs={{0,1},{1,0},{2,3},{3,2},{4,5},{5,4},{6,7},{7,6},{8,9},{9,8},{10,11... | collective-permute-start | bytes 18440 | tf_op jit(solution)/shard_map/ppermute | solution.py:19
  368.0 81.2 %collective-permute-start.36 = (bf16[96,768]{1,0:T(8,128)(2,1)S(1)}, bf16[96,768]{1,0:T(8,128)(2,1)S(1)}, u32[]{:S(2)}, u32[]{:S(2)}) collective-permute-start(bf16[96,768]{1,0:T(8,128)(2,1)S(1)} %constant_dynamic-update-slice_fusion.12), channel_id=1, source_target_pairs={{0,16},{8,24},{16,0},{24,8},{1,17},{9,25},{17,1},{25,9},{2,18},{10... | collective-permute-start | bytes 442376 | tf_op jit(solution)/shard_map/ppermute | solution.py:19
  378.1 26.2 %collective-permute-start.39 = (bf16[192,3072]{1,0:T(8,128)(2,1)S(1)}, bf16[192,3072]{1,0:T(8,128)(2,1)S(1)}, u32[]{:S(2)}, u32[]{:S(2)}) collective-permute-start(bf16[192,3072]{1,0:T(8,128)(2,1)S(1)} %constant_dynamic-slice_fusion.3), channel_id=1, source_target_pairs={{0,1},{1,0},{2,3},{3,2},{4,5},{5,4},{6,7},{7,6},{8,9},{9,8},{10,11... | collective-permute-start | bytes 3538952 | tf_op jit(solution)/shard_map/ppermute | solution.py:19
  390.7 29.0 %collective-permute-start.45 = (bf16[768,768]{1,0:T(8,128)(2,1)S(1)}, bf16[768,768]{1,0:T(8,128)(2,1)S(1)}, u32[]{:S(2)}, u32[]{:S(2)}) collective-permute-start(bf16[768,768]{1,0:T(8,128)(2,1)S(1)} %constant_dynamic-slice_fusion.1), channel_id=1, source_target_pairs={{0,16},{8,24},{16,0},{24,8},{1,17},{9,25},{17,1},{25,9},{2,18},{10... | collective-permute-start | bytes 3538952 | tf_op jit(solution)/shard_map/ppermute | solution.py:19
  404.8 24.3 %collective-permute-start.40 = (bf16[96,3072]{1,0:T(8,128)(2,1)S(1)}, bf16[96,3072]{1,0:T(8,128)(2,1)S(1)}, u32[]{:S(2)}, u32[]{:S(2)}) collective-permute-start(bf16[96,3072]{1,0:T(8,128)(2,1)S(1)} %constant_dynamic-slice_fusion.2), channel_id=1, source_target_pairs={{0,16},{8,24},{16,0},{24,8},{1,17},{9,25},{17,1},{25,9},{2,18},{10... | collective-permute-start | bytes 1769480 | tf_op jit(solution)/shard_map/ppermute | solution.py:19
  406.7 24.6 %collective-permute-start.27 = (bf16[288,384]{1,0:T(8,128)(2,1)S(1)}, bf16[288,384]{1,0:T(8,128)(2,1)S(1)}, u32[]{:S(2)}, u32[]{:S(2)}) collective-permute-start(bf16[288,384]{1,0:T(8,128)(2,1)S(1)} %constant_dynamic-update-slice_fusion.22), channel_id=1, source_target_pairs={{0,2},{2,0},{4,6},{6,4},{1,3},{3,1},{5,7},{7,5},{8,10},{10,8},{12,... | collective-permute-start | bytes 663560 | tf_op jit(solution)/shard_map/ppermute | solution.py:19
  429.5 16.3 %collective-permute-start.41 = (bf16[96,3072]{1,0:T(8,128)(2,1)S(1)}, bf16[96,3072]{1,0:T(8,128)(2,1)S(1)}, u32[]{:S(2)}, u32[]{:S(2)}) collective-permute-start(bf16[96,3072]{1,0:T(8,128)(2,1)S(1)} %get-tuple-element.15), channel_id=1, source_target_pairs={{0,16},{8,24},{16,0},{24,8},{1,17},{9,25},{17,1},{25,9},{2,18},{10... | collective-permute-start | bytes 1769480 | tf_op jit(solution)/shard_map/ppermute | solution.py:19
  431.4 19.3 %collective-permute-start.28 = (bf16[576,384]{1,0:T(8,128)(2,1)S(1)}, bf16[576,384]{1,0:T(8,128)(2,1)S(1)}, u32[]{:S(2)}, u32[]{:S(2)}) collective-permute-start(bf16[576,384]{1,0:T(8,128)(2,1)S(1)} %constant_dynamic-update-slice_fusion.20), channel_id=1, source_target_pairs={{0,16},{8,24},{16,0},{24,8},{1,17},{9,25},{17,1},{25,9},{2,18},{10... | collective-permute-start | bytes 1327112 | tf_op jit(solution)/shard_map/ppermute | solution.py:19
  432.1 18.8 %collective-permute-start.47 = (bf16[384,768]{1,0:T(8,128)(2,1)S(1)}, bf16[384,768]{1,0:T(8,128)(2,1)S(1)}, u32[]{:S(2)}, u32[]{:S(2)}) collective-permute-start(bf16[384,768]{1,0:T(8,128)(2,1)S(1)} %get-tuple-element.13), channel_id=1, source_target_pairs={{0,1},{1,0},{2,3},{3,2},{4,5},{5,4},{6,7},{7,6},{8,9},{9,8},{10,11... | collective-permute-start | bytes 1769480 | tf_op jit(solution)/shard_map/ppermute | solution.py:19
  445.9 22.1 %collective-permute-start.42 = (bf16[192,3072]{1,0:T(8,128)(2,1)S(1)}, bf16[192,3072]{1,0:T(8,128)(2,1)S(1)}, u32[]{:S(2)}, u32[]{:S(2)}) collective-permute-start(bf16[192,3072]{1,0:T(8,128)(2,1)S(1)} %constant_dynamic-update-slice_fusion.6), channel_id=1, source_target_pairs={{0,1},{1,0},{2,3},{3,2},{4,5},{5,4},{6,7},{7,6},{8,9},{9,8},{10,11... | collective-permute-start | bytes 3538952 | tf_op jit(solution)/shard_map/ppermute | solution.py:19
  449.2 19.0 %collective-permute-start.37 = (bf16[192,768]{1,0:T(8,128)(2,1)S(1)}, bf16[192,768]{1,0:T(8,128)(2,1)S(1)}, u32[]{:S(2)}, u32[]{:S(2)}) collective-permute-start(bf16[192,768]{1,0:T(8,128)(2,1)S(1)} %constant_dynamic-update-slice_fusion.10), channel_id=1, source_target_pairs={{0,8},{8,0},{16,24},{24,16},{1,9},{9,1},{17,25},{25,17},{2,10},{10... | collective-permute-start | bytes 884744 | tf_op jit(solution)/shard_map/ppermute | solution.py:19
  450.8 28.8 %collective-permute-start.29 = (bf16[1152,384]{1,0:T(8,128)(2,1)S(1)}, bf16[1152,384]{1,0:T(8,128)(2,1)S(1)}, u32[]{:S(2)}, u32[]{:S(2)}) collective-permute-start(bf16[1152,384]{1,0:T(8,128)(2,1)S(1)} %constant_dynamic-update-slice_fusion.18), channel_id=1, source_target_pairs={{0,8},{8,0},{16,24},{24,16},{1,9},{9,1},{17,25},{25,17},{2,10},{10... | collective-permute-start | bytes 2654216 | tf_op jit(solution)/shard_map/ppermute | solution.py:19
  450.9 28.4 %collective-permute-start.48 = (bf16[768,768]{1,0:T(8,128)(2,1)S(1)}, bf16[768,768]{1,0:T(8,128)(2,1)S(1)}, u32[]{:S(2)}, u32[]{:S(2)}) collective-permute-start(bf16[768,768]{1,0:T(8,128)(2,1)S(1)} %constant_dynamic-update-slice_fusion.2), channel_id=1, source_target_pairs={{0,16},{8,24},{16,0},{24,8},{1,17},{9,25},{17,1},{25,9},{2,18},{10... | collective-permute-start | bytes 3538952 | tf_op jit(solution)/shard_map/ppermute | solution.py:19
  468.1 15.2 %collective-permute-start.43 = (bf16[384,3072]{1,0:T(8,128)(2,1)S(1)}, bf16[384,3072]{1,0:T(8,128)(2,1)S(1)}, u32[]{:S(2)}, u32[]{:S(2)}) collective-permute-start(bf16[384,3072]{1,0:T(8,128)(2,1)S(1)} %constant_dynamic-update-slice_fusion.4), channel_id=1, source_target_pairs={{0,8},{8,0},{16,24},{24,16},{1,9},{9,1},{17,25},{25,17},{2,10},{10... | collective-permute-start | bytes 7077896 | tf_op jit(solution)/shard_map/ppermute | solution.py:19
  (68 other events, 949.0 us)
